TPU v7x, 256 devices: a whole 4x4x8 slice. The times are simulated.
256 devices in a mesh: pipe: 8 (over z_lo, y), expert: 32 (over x, z_hi, core).
Axes of the slice: x: 4, y: 4, z: 8 (z_hi: 4, z_lo: 2; z = z_hi * 2 + z_lo), core: 2. Of those that a mesh axis runs over, the one named last changes fastest.
Arguments:
- hold_a: bfloat16 [8, 1024, 3584], P('pipe', 'expert'), may hold values from -48 to 48
- enter_a: bfloat16 [1024, 3584], P('expert'), may hold values from -48 to 48
- saved_b: bfloat16 [2, 8, 1024, 3584], P(None, 'pipe', 'expert'), may hold values from -48 to 48
- hold_g: bfloat16 [8, 1024, 3584], P('pipe', 'expert'), may hold values from -6 to 6
- enter_g: bfloat16 [1024, 3584], P('expert'), may hold values from -6 to 6
- gain: bfloat16 [8, 3584], P('pipe'), may hold values from 0.099609375 to 1.8984375
- w_gate: bfloat16 [8, 3584, 16384], P('pipe', None, 'expert'), may hold values from -0.09375 to 0.09375
- w_up: bfloat16 [8, 3584, 16384], P('pipe', None, 'expert'), may hold values from -0.09375 to 0.09375
- w_down: bfloat16 [8, 16384, 3584], P('pipe', 'expert'), may hold values from -0.1875 to 0.1875
- route_a: int32 [2, 8, 1024, 2], P(None, 'pipe', 'expert'), may hold values from 0 to 15, all different within a row; in each aligned block of 32 rows (0 to 31, 32 to 63, ..., all dimensions but the last counted through in order) at most 6 rows name the same one
- gate_a: int32 [2, 8, 1024, 2], P(None, 'pipe', 'expert'), may hold values from 16 to 255
- route_b: int32 [2, 8, 1024, 2], P(None, 'pipe', 'expert'), may hold values from 0 to 15, all different within a row; in each aligned block of 32 rows (0 to 31, 32 to 63, ..., all dimensions but the last counted through in order) at most 6 rows name the same one
- gate_b: int32 [2, 8, 1024, 2], P(None, 'pipe', 'expert'), may hold values from 16 to 255
Outputs:
- made_out: bfloat16 [2, 8, 1024, 3584], P(None, 'pipe', 'expert')
- grad_out: bfloat16 [2, 8, 1024, 3584], P(None, 'pipe', 'expert')
Inputs may be any that keep to these rules, and one draw needn't show every extreme that they name: `route_a`: each row names 2 different experts. Within the 32 rows of one device, for one step and layer, no expert is named more than 6 times, and that count is reached. `route_b`: each row names 2 different experts. Within the 32 rows of one device, for one step and layer, no expert is named more than 6 times, and that count is reached.
All inputs are finite; a program needn't handle non-finite values.
Results may differ from a plain program's by a relative error of at most 0.015.
Values may be sent and summed in bfloat16 or wider, within the bound.
A program may use at most 128 MiB of HBM per device.

v0:
```python
import jax
import jax.numpy as jnp
from jax import lax
from jax.sharding import PartitionSpec as P

SLICES = 2
TOP = 2
TICKS = 2


epsilon = 1e-06
gate_unit = 1.0 / 256.0


def from_behind(block, axis, distance):
    devices = range(lax.axis_size(axis))
    route = [(i - distance, i) for i in devices if i - distance in devices]
    return lax.ppermute(block, axis, route)


def norm_rows(x_rows, gain_row):
    as_float = x_rows.astype(jnp.float32)
    inverse = lax.rsqrt(jnp.mean(as_float * as_float, axis=1, keepdims=True) + epsilon)
    normed = (as_float * inverse * gain_row.astype(jnp.float32)[None, :]).astype(jnp.bfloat16)
    return (as_float, inverse, normed)


def slot_tables(route, experts, capacity, slices):
    flat_route = route.reshape(-1)
    matches = (flat_route[:, None] == jnp.arange(experts, dtype=jnp.int32)[None, :]).astype(
        jnp.int32
    )
    position = jnp.sum((jnp.cumsum(matches, axis=0) - matches) * matches, axis=1)
    quarter = capacity // slices
    home_slot = flat_route * capacity + position
    split_slot = (
        position // quarter * (experts * quarter) + flat_route * quarter + position % quarter
    )
    return (home_slot, split_slot)


def forward_kernel(flat_rows, weights):
    gate_pre = jnp.dot(flat_rows[0], weights[0], preferred_element_type=jnp.float32)
    up_pre = jnp.dot(flat_rows[0], weights[1], preferred_element_type=jnp.float32)
    hidden = (gate_pre * jax.nn.sigmoid(gate_pre) * up_pre).astype(jnp.bfloat16)
    return jnp.dot(hidden, weights[2], preferred_element_type=jnp.float32).astype(jnp.bfloat16)


def backward_kernel(flat_rows, weights):
    contract = (((1,), (1,)), ((), ()))
    gate_pre = jnp.dot(flat_rows[0], weights[0], preferred_element_type=jnp.float32)
    up_pre = jnp.dot(flat_rows[0], weights[1], preferred_element_type=jnp.float32)
    sigma_gate = jax.nn.sigmoid(gate_pre)
    grad_hidden = lax.dot_general(
        flat_rows[1], weights[2], contract, preferred_element_type=jnp.float32
    )
    grad_gate = (grad_hidden * up_pre * sigma_gate * (1.0 + gate_pre * (1.0 - sigma_gate))).astype(
        jnp.bfloat16
    )
    grad_up = (grad_hidden * gate_pre * sigma_gate).astype(jnp.bfloat16)
    from_gate = lax.dot_general(grad_gate, weights[0], contract, preferred_element_type=jnp.float32)
    from_up = lax.dot_general(grad_up, weights[1], contract, preferred_element_type=jnp.float32)
    return (from_gate + from_up).astype(jnp.bfloat16)


def run_experts(pieces, home_slot, experts, capacity, kernel, weights):
    devices = lax.axis_size("expert")
    slices = devices // experts
    feature_count = pieces[0].shape[1]
    slot_ids = jnp.arange(experts * capacity, dtype=jnp.int32)[:, None]
    select = (home_slot[None, :] == slot_ids).astype(jnp.bfloat16)
    buffers = tuple(
        (
            jnp.broadcast_to(
                jnp.dot(select, piece, preferred_element_type=jnp.float32)
                .astype(jnp.bfloat16)
                .reshape(1, experts * capacity, feature_count),
                (slices, experts * capacity, feature_count),
            ).reshape(devices, capacity, feature_count)
            for piece in pieces
        )
    )
    if len(buffers) == 1:
        arrived = (lax.all_to_all(buffers[0], "expert", split_axis=0, concat_axis=0, tiled=True),)
    else:
        arrived = (
            lax.all_to_all(buffers[0], "expert", split_axis=0, concat_axis=0, tiled=True),
            lax.all_to_all(buffers[1], "expert", split_axis=0, concat_axis=0, tiled=True),
        )
    flat_rows = tuple((item.reshape(devices * capacity, feature_count) for item in arrived))
    partial_value = kernel(flat_rows, weights).reshape(devices, capacity, feature_count)
    returned = lax.all_to_all(partial_value, "expert", split_axis=0, concat_axis=0, tiled=True)
    return jnp.sum(
        returned.reshape(slices, experts * capacity, feature_count).astype(jnp.float32), axis=0
    )


def slot_matrix(home_slot, tokens, experts, capacity, scale_rows):
    slot_ids = jnp.arange(experts * capacity, dtype=jnp.int32)[None, None, :]
    hits = (home_slot.reshape(tokens, -1)[:, :, None] == slot_ids).astype(jnp.float32)
    return jnp.sum(hits * scale_rows[:, :, None], axis=1)


def layer_forward(x_rows, gain_row, weights, route, gate_num, experts, capacity):
    as_float, inverse, normed = norm_rows(x_rows, gain_row)
    tokens, choose_count = route.shape
    home_slot, split_slot = slot_tables(
        route, experts, capacity, lax.axis_size("expert") // experts
    )
    token_rows = jnp.repeat(normed, choose_count, axis=0)
    summed = run_experts((token_rows,), home_slot, experts, capacity, forward_kernel, weights)
    gate_value = gate_num.astype(jnp.float32) * gate_unit
    mixer = slot_matrix(home_slot, tokens, experts, capacity, gate_value)
    branch = jnp.dot(mixer, summed, precision=lax.Precision.HIGHEST)
    return (as_float + branch).astype(jnp.bfloat16)


def layer_backward(x_rows, cot, gain_row, weights, route, gate_num, experts, capacity):
    as_float, inverse, normed = norm_rows(x_rows, gain_row)
    tokens, choose_count = route.shape
    home_slot, split_slot = slot_tables(
        route, experts, capacity, lax.axis_size("expert") // experts
    )
    token_rows = jnp.repeat(normed, choose_count, axis=0)
    gate_value = gate_num.astype(jnp.float32) * gate_unit
    cot_float = cot.astype(jnp.float32)
    cot_rows = (
        (gate_value[:, :, None] * cot_float[:, None, :])
        .astype(jnp.bfloat16)
        .reshape(tokens * choose_count, -1)
    )
    summed = run_experts(
        (token_rows, cot_rows), home_slot, experts, capacity, backward_kernel, weights
    )
    picker = slot_matrix(home_slot, tokens, experts, capacity, jnp.ones_like(gate_value))
    d_normed = jnp.dot(picker, summed, precision=lax.Precision.HIGHEST)
    gained = gain_row.astype(jnp.float32)[None, :] * d_normed
    inner = jnp.mean(as_float * gained, axis=1, keepdims=True)
    grad_x = cot_float + inverse * gained - as_float * inverse**3 * inner
    return grad_x.astype(jnp.bfloat16)


def body(
    hold_a,
    enter_a,
    saved_b,
    hold_g,
    enter_g,
    gain,
    w_gate,
    w_up,
    w_down,
    route_a,
    gate_a,
    route_b,
    gate_b,
):
    devices = lax.axis_size("expert")
    experts = devices // SLICES
    tokens = hold_a.shape[1]
    capacity = min(
        tokens, SLICES * ((3 * tokens * TOP + 2 * experts * SLICES - 1) // (2 * experts * SLICES))
    )
    sections = lax.axis_size("pipe")
    section_index = lax.axis_index("pipe")
    weights = (w_gate[0], w_up[0], w_down[0])
    gain_row = gain[0]
    forward_in = hold_a[0]
    cot_in = hold_g[0]
    made_list = []
    grad_list = []
    for tick_index in range(TICKS):
        layer_out = layer_forward(
            forward_in,
            gain_row,
            weights,
            route_a[tick_index, 0],
            gate_a[tick_index, 0],
            experts,
            capacity,
        )
        grad_in = layer_backward(
            saved_b[tick_index, 0],
            cot_in,
            gain_row,
            weights,
            route_b[tick_index, 0],
            gate_b[tick_index, 0],
            experts,
            capacity,
        )
        made_list.append(layer_out)
        grad_list.append(grad_in)
        if tick_index + 1 < TICKS:
            shifted = from_behind(layer_out, "pipe", 1)
            forward_in = jnp.where(section_index == 0, enter_a, shifted)
            lowered = from_behind(grad_in, "pipe", -1)
            cot_in = jnp.where(section_index == sections - 1, enter_g, lowered)
    return (jnp.stack(made_list)[:, None], jnp.stack(grad_list)[:, None])


def solution(mesh):
    placed = (
        P("pipe", "expert", None),
        P("expert", None),
        P(None, "pipe", "expert", None),
        P("pipe", "expert", None),
        P("expert", None),
        P("pipe", None),
        P("pipe", None, "expert"),
        P("pipe", None, "expert"),
        P("pipe", "expert", None),
        P(None, "pipe", "expert", None),
        P(None, "pipe", "expert", None),
        P(None, "pipe", "expert", None),
        P(None, "pipe", "expert", None),
    )
    return jax.shard_map(
        body,
        mesh=mesh,
        in_specs=placed,
        out_specs=(P(None, "pipe", "expert", None), P(None, "pipe", "expert", None)),
        check_vma=False,
    )
```

profile of v0, /device:TPU:1, one launch (start us, length us, event | category | flops | bytes accessed | tf_op | source)
XLA Modules:
  0.0 542.5 jit_solution(15481335591148180975)
XLA Ops:
  6.1 12.7 %all-to-all-start.4 = ((bf16[32,6,3584]{2,1,0:T(8,128)(2,1)}), bf16[32,6,3584]{2,1,0:T(8,128)(2,1)S(1)}, u32[]{:S(2)}, u32[]{:S(2)}) async-start(bf16[32,6,3584]{2,1,0:T(8,128)(2,1)} %reshape.290), calls=%async_computation.4 | async-start | bytes 3670016 | tf_op jit(solution)/shard_map/all_to_all | solution.py:88
  26.5 37.5 %all-to-all-done.4 = bf16[32,6,3584]{2,1,0:T(8,128)(2,1)S(1)} async-done(((bf16[32,6,3584]{2,1,0:T(8,128)(2,1)}), bf16[32,6,3584]{2,1,0:T(8,128)(2,1)S(1)}, u32[]{:S(2)}, u32[]{:S(2)}) %all-to-all-start.4) | async-done | bytes 1376288 | tf_op jit(solution)/shard_map/all_to_all | solution.py:88
  64.0 6.5 %all-to-all-start.5 = ((bf16[32,6,3584]{2,1,0:T(8,128)(2,1)}), bf16[32,6,3584]{2,1,0:T(8,128)(2,1)}, u32[]{:S(2)}, u32[]{:S(2)}) async-start(bf16[32,6,3584]{2,1,0:T(8,128)(2,1)} %reshape.293), calls=%async_computation.5 | async-start | bytes 3670016 | tf_op jit(solution)/shard_map/all_to_all | solution.py:87
  78.2 37.6 %all-to-all-done.5 = bf16[32,6,3584]{2,1,0:T(8,128)(2,1)} async-done(((bf16[32,6,3584]{2,1,0:T(8,128)(2,1)}), bf16[32,6,3584]{2,1,0:T(8,128)(2,1)}, u32[]{:S(2)}, u32[]{:S(2)}) %all-to-all-start.5) | async-done | bytes 1376288 | tf_op jit(solution)/shard_map/all_to_all | solution.py:87
  115.8 6.7 %all-to-all-start = ((bf16[32,6,3584]{2,1,0:T(8,128)(2,1)}), bf16[32,6,3584]{2,1,0:T(8,128)(2,1)}, u32[]{:S(2)}, u32[]{:S(2)}) async-start(bf16[32,6,3584]{2,1,0:T(8,128)(2,1)} %reshape.283), calls=%async_computation | async-start | bytes 3670016 | tf_op jit(solution)/shard_map/all_to_all | solution.py:84
  131.2 6.8 %fusion.25 = f32[192,3584]{1,0:T(8,128)} fusion(bf16[1,3584,512]{2,1,0:T(8,128)(2,1)} %param.19, f32[192,512]{1,0:T(8,128)S(1)} %fusion.7, bf16[192,3584]{1,0:T(8,128)(2,1)S(1)} %reshape.294, bf16[1,3584,512]{2,1,0:T(8,128)(2,1)} %param.20, f32[192,512]{1,0:T(8,128)S(1)} %fusion.27), kind=kOutput, calls=%fused_computation.39 | convolution fusion | flops 1410269184 | bytes 12255232 | tf_op jit(solution)/shard_map/dot_general | solution.py:61
  143.8 24.4 %all-to-all-done = bf16[32,6,3584]{2,1,0:T(8,128)(2,1)} async-done(((bf16[32,6,3584]{2,1,0:T(8,128)(2,1)}), bf16[32,6,3584]{2,1,0:T(8,128)(2,1)}, u32[]{:S(2)}, u32[]{:S(2)}) %all-to-all-start) | async-done | bytes 1376288 | tf_op jit(solution)/shard_map/all_to_all | solution.py:84
  179.8 6.4 %convolution_convert_fusion.1 = bf16[192,3584]{1,0:T(8,128)(2,1)} fusion(bf16[1,512,3584]{2,1,0:T(8,128)(2,1)} %param.21, bf16[192,3584]{1,0:T(8,128)(2,1)} %reshape.284, bf16[1,3584,512]{2,1,0:T(8,128)(2,1)} %param.20, f32[192,512]{1,0:T(8,128)S(1)} %fusion.31), kind=kOutput, calls=%fused_computation.5 | convolution fusion | flops 1410564096 | bytes 10485760 | tf_op jit(solution)/shard_map/dot_general | solution.py:46
  189.6 29.1 %all-to-all-done.6 = bf16[32,6,3584]{2,1,0:T(8,128)(2,1)S(1)} async-done(((bf16[32,6,3584]{2,1,0:T(8,128)(2,1)}), bf16[32,6,3584]{2,1,0:T(8,128)(2,1)S(1)}, u32[]{:S(2)}, u32[]{:S(2)}) %all-to-all-start.6) | async-done | bytes 1376288 | tf_op jit(solution)/shard_map/all_to_all | solution.py:92
  218.7 5.0 all-to-all-start.1
  229.6 40.6 %all-to-all-done.1 = bf16[32,6,3584]{2,1,0:T(8,128)(2,1)} async-done(((bf16[32,6,3584]{2,1,0:T(8,128)(2,1)}), bf16[32,6,3584]{2,1,0:T(8,128)(2,1)}, u32[]{:S(2)}, u32[]{:S(2)}) %all-to-all-start.1) | async-done | bytes 1376288 | tf_op jit(solution)/shard_map/all_to_all | solution.py:92
  285.9 5.7 %all-to-all-start.2 = ((bf16[32,6,3584]{2,1,0:T(8,128)(2,1)}), bf16[32,6,3584]{2,1,0:T(8,128)(2,1)S(1)}, u32[]{:S(2)}, u32[]{:S(2)}) async-start(bf16[32,6,3584]{2,1,0:T(8,128)(2,1)} %reshape.287), calls=%async_computation.2 | async-start | bytes 3670016 | tf_op jit(solution)/shard_map/all_to_all | solution.py:84
  294.0 35.9 %all-to-all-done.2 = bf16[32,6,3584]{2,1,0:T(8,128)(2,1)S(1)} async-done(((bf16[32,6,3584]{2,1,0:T(8,128)(2,1)}), bf16[32,6,3584]{2,1,0:T(8,128)(2,1)S(1)}, u32[]{:S(2)}, u32[]{:S(2)}) %all-to-all-start.2) | async-done | bytes 1376288 | tf_op jit(solution)/shard_map/all_to_all | solution.py:84
  329.9 12.5 %all-to-all-start.8 = ((bf16[32,6,3584]{2,1,0:T(8,128)(2,1)}), bf16[32,6,3584]{2,1,0:T(8,128)(2,1)}, u32[]{:S(2)}, u32[]{:S(2)}) async-start(bf16[32,6,3584]{2,1,0:T(8,128)(2,1)} %reshape.299), calls=%async_computation.8 | async-start | bytes 3670016 | tf_op jit(solution)/shard_map/all_to_all | solution.py:87
  343.9 7.9 %collective-permute-done.1 = bf16[32,3584]{1,0:T(8,128)(2,1)S(1)} collective-permute-done((bf16[32,3584]{1,0:T(8,128)(2,1)S(1)}, bf16[32,3584]{1,0:T(8,128)(2,1)S(1)}, u32[]{:S(2)}, u32[]{:S(2)}) %collective-permute-start.1) | collective-permute-done | bytes 229408 | tf_op jit(solution)/shard_map/ppermute | solution.py:18
  357.6 23.5 %all-to-all-done.8 = bf16[32,6,3584]{2,1,0:T(8,128)(2,1)} async-done(((bf16[32,6,3584]{2,1,0:T(8,128)(2,1)}), bf16[32,6,3584]{2,1,0:T(8,128)(2,1)}, u32[]{:S(2)}, u32[]{:S(2)}) %all-to-all-start.8) | async-done | bytes 1376288 | tf_op jit(solution)/shard_map/all_to_all | solution.py:87
  381.2 12.3 %all-to-all-start.7 = ((bf16[32,6,3584]{2,1,0:T(8,128)(2,1)}), bf16[32,6,3584]{2,1,0:T(8,128)(2,1)}, u32[]{:S(2)}, u32[]{:S(2)}) async-start(bf16[32,6,3584]{2,1,0:T(8,128)(2,1)} %reshape.296), calls=%async_computation.7 | async-start | bytes 3670016 | tf_op jit(solution)/shard_map/all_to_all | solution.py:88
  396.9 4.9 convolution_convert_fusion
  403.2 28.7 %all-to-all-done.7 = bf16[32,6,3584]{2,1,0:T(8,128)(2,1)} async-done(((bf16[32,6,3584]{2,1,0:T(8,128)(2,1)}), bf16[32,6,3584]{2,1,0:T(8,128)(2,1)}, u32[]{:S(2)}, u32[]{:S(2)}) %all-to-all-start.7) | async-done | bytes 1376288 | tf_op jit(solution)/shard_map/all_to_all | solution.py:88
  431.9 12.7 %all-to-all-start.3 = ((bf16[32,6,3584]{2,1,0:T(8,128)(2,1)}), bf16[32,6,3584]{2,1,0:T(8,128)(2,1)S(1)}, u32[]{:S(2)}, u32[]{:S(2)}) async-start(bf16[32,6,3584]{2,1,0:T(8,128)(2,1)} %reshape.289), calls=%async_computation.3 | async-start | bytes 3670016 | tf_op jit(solution)/shard_map/all_to_all | solution.py:92
  458.8 7.1 %fusion.21 = f32[192,3584]{1,0:T(8,128)} fusion(bf16[1,3584,512]{2,1,0:T(8,128)(2,1)} %param.19, f32[192,512]{1,0:T(8,128)} %fusion.5, bf16[192,3584]{1,0:T(8,128)(2,1)S(1)} %reshape.300, bf16[1,3584,512]{2,1,0:T(8,128)(2,1)} %param.20, f32[192,512]{1,0:T(8,128)} %fusion.23), kind=kOutput, calls=%fused_computation.35 | convolution fusion | flops 1410269184 | bytes 12255232 | tf_op jit(solution)/shard_map/dot_general | solution.py:61
  471.8 11.7 %all-to-all-done.3 = bf16[32,6,3584]{2,1,0:T(8,128)(2,1)S(1)} async-done(((bf16[32,6,3584]{2,1,0:T(8,128)(2,1)}), bf16[32,6,3584]{2,1,0:T(8,128)(2,1)S(1)}, u32[]{:S(2)}, u32[]{:S(2)}) %all-to-all-start.3) | async-done | bytes 1376288 | tf_op jit(solution)/shard_map/all_to_all | solution.py:92
  484.8 11.9 %all-to-all-start.9 = ((bf16[32,6,3584]{2,1,0:T(8,128)(2,1)}), bf16[32,6,3584]{2,1,0:T(8,128)(2,1)}, u32[]{:S(2)}, u32[]{:S(2)}) async-start(bf16[32,6,3584]{2,1,0:T(8,128)(2,1)} %reshape.301), calls=%async_computation.9 | async-start | bytes 3670016 | tf_op jit(solution)/shard_map/all_to_all | solution.py:92
  503.7 31.7 %all-to-all-done.9 = bf16[32,6,3584]{2,1,0:T(8,128)(2,1)} async-done(((bf16[32,6,3584]{2,1,0:T(8,128)(2,1)}), bf16[32,6,3584]{2,1,0:T(8,128)(2,1)}, u32[]{:S(2)}, u32[]{:S(2)}) %all-to-all-start.9) | async-done | bytes 1376288 | tf_op jit(solution)/shard_map/all_to_all | solution.py:92
  (168 shorter events, 121.4 us)
Async XLA Ops:
  6.1 12.7 %copy-start.16 = (bf16[1,3584]{1,0:T(2,128)(2,1)S(1)}, bf16[1,3584]{1,0:T(2,128)(2,1)}, u32[]{:S(2)}) copy-start(bf16[1,3584]{1,0:T(2,128)(2,1)} %param.18) | copy-start | bytes 21508
  6.1 12.8 %copy-start.8 = (bf16[1,32,3584]{2,1,0:T(8,128)(2,1)S(1)}, bf16[1,32,3584]{2,1,0:T(8,128)(2,1)}, u32[]{:S(2)}) copy-start(bf16[1,32,3584]{2,1,0:T(8,128)(2,1)} %param.13) | copy-start | bytes 688132
  6.1 13.0 %copy-start.3 = (bf16[2,1,32,3584]{3,2,1,0:T(8,128)(2,1)S(1)}, bf16[2,1,32,3584]{3,2,1,0:T(8,128)(2,1)}, u32[]{:S(2)}) copy-start(bf16[2,1,32,3584]{3,2,1,0:T(8,128)(2,1)} %param.15) | copy-start | bytes 1376260
  6.1 57.9 %all-to-all-start.4 = ((bf16[32,6,3584]{2,1,0:T(8,128)(2,1)}), bf16[32,6,3584]{2,1,0:T(8,128)(2,1)S(1)}, u32[]{:S(2)}, u32[]{:S(2)}) async-start(bf16[32,6,3584]{2,1,0:T(8,128)(2,1)} %reshape.290), calls=%async_computation.4 | async-start | bytes 3670016 | tf_op jit(solution)/shard_map/all_to_all | solution.py:88
  26.5 44.0 %copy-start.18 = (s32[2,1,32,2]{2,3,1,0:T(2,128)S(1)}, s32[2,1,32,2]{2,3,1,0:T(2,128)}, u32[]{:S(2)}) copy-start(s32[2,1,32,2]{2,3,1,0:T(2,128)} %param.22) | copy-start | bytes 1540
  64.0 51.8 %all-to-all-start.5 = ((bf16[32,6,3584]{2,1,0:T(8,128)(2,1)}), bf16[32,6,3584]{2,1,0:T(8,128)(2,1)}, u32[]{:S(2)}, u32[]{:S(2)}) async-start(bf16[32,6,3584]{2,1,0:T(8,128)(2,1)} %reshape.293), calls=%async_computation.5 | async-start | bytes 3670016 | tf_op jit(solution)/shard_map/all_to_all | solution.py:87
  115.8 52.4 %all-to-all-start = ((bf16[32,6,3584]{2,1,0:T(8,128)(2,1)}), bf16[32,6,3584]{2,1,0:T(8,128)(2,1)}, u32[]{:S(2)}, u32[]{:S(2)}) async-start(bf16[32,6,3584]{2,1,0:T(8,128)(2,1)} %reshape.283), calls=%async_computation | async-start | bytes 3670016 | tf_op jit(solution)/shard_map/all_to_all | solution.py:84
  168.2 50.5 %all-to-all-start.6 = ((bf16[32,6,3584]{2,1,0:T(8,128)(2,1)}), bf16[32,6,3584]{2,1,0:T(8,128)(2,1)S(1)}, u32[]{:S(2)}, u32[]{:S(2)}) async-start(bf16[32,6,3584]{2,1,0:T(8,128)(2,1)} %reshape.295), calls=%async_computation.6 | async-start | bytes 3670016 | tf_op jit(solution)/shard_map/all_to_all | solution.py:92
  189.6 36.0 %copy-start.17 = (s32[2,1,32,2]{2,3,1,0:T(2,128)S(1)}, s32[2,1,32,2]{2,3,1,0:T(2,128)}, u32[]{:S(2)}) copy-start(s32[2,1,32,2]{2,3,1,0:T(2,128)} %param.24) | copy-start | bytes 1540
  189.6 36.1 %copy-start.20 = (s32[2,1,32,2]{2,3,1,0:T(2,128)S(1)}, s32[2,1,32,2]{2,3,1,0:T(2,128)}, u32[]{:S(2)}) copy-start(s32[2,1,32,2]{2,3,1,0:T(2,128)} %param.23) | copy-start | bytes 1540
  218.7 5.1 copy-start.1
  218.7 51.5 %all-to-all-start.1 = ((bf16[32,6,3584]{2,1,0:T(8,128)(2,1)}), bf16[32,6,3584]{2,1,0:T(8,128)(2,1)}, u32[]{:S(2)}, u32[]{:S(2)}) async-start(bf16[32,6,3584]{2,1,0:T(8,128)(2,1)} %reshape.285), calls=%async_computation.1 | async-start | bytes 3670016 | tf_op jit(solution)/shard_map/all_to_all | solution.py:92
  273.9 8.5 %copy-start.15 = (bf16[32,3584]{1,0:T(8,128)(2,1)S(1)}, bf16[32,3584]{1,0:T(8,128)(2,1)}, u32[]{:S(2)}) copy-start(bf16[32,3584]{1,0:T(8,128)(2,1)} %param.14) | copy-start | bytes 688132
  276.2 7.5 %copy-start.9 = (bf16[32,3584]{1,0:T(8,128)(2,1)}, bf16[32,3584]{1,0:T(8,128)(2,1)S(1)}, u32[]{:S(2)}) copy-start(bf16[32,3584]{1,0:T(8,128)(2,1)S(1)} %fusion.2) | copy-start | bytes 688132
  276.2 6.5 %copy-start.13 = (bf16[1,32,3584]{2,1,0:T(8,128)(2,1)S(1)}, bf16[1,32,3584]{2,1,0:T(8,128)(2,1)}, u32[]{:S(2)}) copy-start(bf16[1,32,3584]{2,1,0:T(8,128)(2,1)} %param.16) | copy-start | bytes 688132
  276.2 6.3 %collective-permute-start = (bf16[32,3584]{1,0:T(8,128)(2,1)S(1)}, bf16[32,3584]{1,0:T(8,128)(2,1)S(1)}, u32[]{:S(2)}, u32[]{:S(2)}) collective-permute-start(bf16[32,3584]{1,0:T(8,128)(2,1)S(1)} %fusion.2), channel_id=1, source_target_pairs={{0,32},{32,64},{64,96},{96,128},{128,160},{160,192},{192,224},{1,3... | collective-permute-start | bytes 688136 | tf_op jit(solution)/shard_map/ppermute | solution.py:18
  285.9 44.0 %all-to-all-start.2 = ((bf16[32,6,3584]{2,1,0:T(8,128)(2,1)}), bf16[32,6,3584]{2,1,0:T(8,128)(2,1)S(1)}, u32[]{:S(2)}, u32[]{:S(2)}) async-start(bf16[32,6,3584]{2,1,0:T(8,128)(2,1)} %reshape.287), calls=%async_computation.2 | async-start | bytes 3670016 | tf_op jit(solution)/shard_map/all_to_all | solution.py:84
  294.0 48.4 %copy-start.11 = (bf16[32,3584]{1,0:T(8,128)(2,1)S(1)}, bf16[32,3584]{1,0:T(8,128)(2,1)}, u32[]{:S(2)}) copy-start(bf16[32,3584]{1,0:T(8,128)(2,1)} %get-tuple-element.13) | copy-start | bytes 688132
  294.0 57.8 %copy-start.14 = (bf16[32,3584]{1,0:T(8,128)(2,1)S(1)}, bf16[32,3584]{1,0:T(8,128)(2,1)}, u32[]{:S(2)}) copy-start(bf16[32,3584]{1,0:T(8,128)(2,1)} %param.17) | copy-start | bytes 688132
  329.9 51.3 %all-to-all-start.8 = ((bf16[32,6,3584]{2,1,0:T(8,128)(2,1)}), bf16[32,6,3584]{2,1,0:T(8,128)(2,1)}, u32[]{:S(2)}, u32[]{:S(2)}) async-start(bf16[32,6,3584]{2,1,0:T(8,128)(2,1)} %reshape.299), calls=%async_computation.8 | async-start | bytes 3670016 | tf_op jit(solution)/shard_map/all_to_all | solution.py:87
  342.4 9.4 %collective-permute-start.1 = (bf16[32,3584]{1,0:T(8,128)(2,1)S(1)}, bf16[32,3584]{1,0:T(8,128)(2,1)S(1)}, u32[]{:S(2)}, u32[]{:S(2)}) collective-permute-start(bf16[32,3584]{1,0:T(8,128)(2,1)S(1)} %copy-done.11), channel_id=1, source_target_pairs={{32,0},{64,32},{96,64},{128,96},{160,128},{192,160},{224,192},{33,... | collective-permute-start | bytes 688136 | tf_op jit(solution)/shard_map/ppermute | solution.py:18
  381.2 50.8 %all-to-all-start.7 = ((bf16[32,6,3584]{2,1,0:T(8,128)(2,1)}), bf16[32,6,3584]{2,1,0:T(8,128)(2,1)}, u32[]{:S(2)}, u32[]{:S(2)}) async-start(bf16[32,6,3584]{2,1,0:T(8,128)(2,1)} %reshape.296), calls=%async_computation.7 | async-start | bytes 3670016 | tf_op jit(solution)/shard_map/all_to_all | solution.py:88
  431.9 51.6 %all-to-all-start.3 = ((bf16[32,6,3584]{2,1,0:T(8,128)(2,1)}), bf16[32,6,3584]{2,1,0:T(8,128)(2,1)S(1)}, u32[]{:S(2)}, u32[]{:S(2)}) async-start(bf16[32,6,3584]{2,1,0:T(8,128)(2,1)} %reshape.289), calls=%async_computation.3 | async-start | bytes 3670016 | tf_op jit(solution)/shard_map/all_to_all | solution.py:92
  484.8 50.6 %all-to-all-start.9 = ((bf16[32,6,3584]{2,1,0:T(8,128)(2,1)}), bf16[32,6,3584]{2,1,0:T(8,128)(2,1)}, u32[]{:S(2)}, u32[]{:S(2)}) async-start(bf16[32,6,3584]{2,1,0:T(8,128)(2,1)} %reshape.301), calls=%async_computation.9 | async-start | bytes 3670016 | tf_op jit(solution)/shard_map/all_to_all | solution.py:92
  (9 other events, 20.0 us)
where the time goes:
time: 553 us; the launch traced here: 543 us
  waiting for transfers between devices  313 us (57%)
  starting transfers between devices  93.4 us (17%)
  matrix products  64.8 us (12%)
  local copies, waits for them, and re-layouts  58.5 us (11%)
  other arithmetic  11.9 us (2%)
    all_to_all x4, waiting for transfers between devices, run_experts(): lax.all_to_all(buffers[0], 'expert', split_axis=0, concat_axis=0, tiled=T...  121 us
    all_to_all x4, waiting for transfers between devices, run_experts(): lax.all_to_all(partial_value, 'expert', split_axis=0, concat_axis=0, tile...  113 us
    all_to_all x2, waiting for transfers between devices, run_experts(): lax.all_to_all(buffers[1], 'expert', split_axis=0, concat_axis=0, tiled=T...  66.2 us
    all_to_all x4, starting transfers between devices, run_experts(): lax.all_to_all(partial_value, 'expert', split_axis=0, concat_axis=0, tile...  34.3 us
    all_to_all x4, starting transfers between devices, run_experts(): lax.all_to_all(buffers[0], 'expert', split_axis=0, concat_axis=0, tiled=T...  31.3 us
    all_to_all x2, starting transfers between devices, run_experts(): lax.all_to_all(buffers[1], 'expert', split_axis=0, concat_axis=0, tiled=T...  25 us
    dot_general x2, matrix products, backward_kernel(): lax.dot_general(grad_gate, weights[0], contract, preferred_element_type=j...  13.9 us
    reshape x6, local copies, waits for them, and re-layouts, run_experts(): item.reshape(devices * capacity, feature_count)  13.8 us
  transfers between devices with their start and end apart: 12, of which 12 were waited for; matrix products, arithmetic and copies ran while one was open for 21% of the time, Pallas kernels for 0%

commit v1 on v0

v1 whole, which is shorter than its diff:
```python
import functools

import jax
import jax.numpy as jnp
import numpy as np
from jax import lax
from jax.experimental import pallas as pl
from jax.experimental.pallas import tpu as pltpu
from jax.sharding import PartitionSpec as P

SLICES = 2
TOP = 2
TICKS = 2
CAP = 6
MESH = pl.DeviceIdType.MESH
BF = jnp.bfloat16
F32 = jnp.float32

epsilon = 1e-06
gate_unit = 1.0 / 256.0

XN = 4
ZN = 4
PEERS = 8
GROUPS = 4
SLOTS = 48
COL = 128
PART = GROUPS * COL
LAG = 2


def perm_tables():
    r, g, q, s = np.meshgrid(
        np.arange(PEERS), np.arange(GROUPS), np.arange(2), np.arange(CAP), indexing="ij"
    )
    r, g, q, s = (a.reshape(-1) for a in (r, g, q, s))
    zrow = r * SLOTS + g * 2 * CAP + q * CAP + s
    p1 = np.zeros((PEERS * SLOTS, PEERS * SLOTS), np.float32)
    p1[g * 2 * SLOTS + q * SLOTS + r * CAP + s, zrow] = 1.0
    p2 = np.zeros((PEERS * SLOTS, GROUPS * XN * SLOTS), np.float32)
    for dx in range(XN):
        hit = q == dx % 2
        p2[zrow[hit], (g * XN * SLOTS + dx * SLOTS + r * CAP + s)[hit]] = 1.0
    return p1, p2


def place_of(index):
    return index // (ZN * 2), (index // 2) % ZN, index % 2


def route_tables(route, gate):
    number, tokens, top = route.shape
    experts = ZN * 2 * 2
    x, z, c = place_of(lax.axis_index("expert"))
    flat = route.reshape(number, tokens * top)
    matches = (flat[:, :, None] == jnp.arange(experts, dtype=jnp.int32)).astype(jnp.int32)
    before = jnp.cumsum(matches, axis=1) - matches
    slot = flat * CAP + jnp.sum(before * matches, axis=2)
    slot = slot.reshape(number, tokens, top)
    row = np.arange(PEERS * SLOTS)
    r, g, q, s = row // SLOTS, row // (2 * CAP) % GROUPS, row // CAP % 2, row % CAP
    expert = (x + q) % 2 * (ZN * 2) + (z + r // 2) % ZN * 2 + (c + r % 2) % 2
    row_slot = (expert * CAP + s).astype(jnp.int32)
    own_group = (g[:, None] == np.arange(GROUPS * tokens)[None, :] // tokens)
    lanes = jnp.tile(slot.transpose(0, 2, 1), (1, 1, GROUPS))
    gate_lanes = jnp.tile(gate.transpose(0, 2, 1).astype(F32) * gate_unit, (1, 1, GROUPS))
    hit = (lanes[:, :, None, :] == row_slot[None, None, :, None]) & own_group[None, None]
    plain = jnp.sum(hit.astype(F32), axis=1).astype(BF)
    gated = jnp.sum(jnp.where(hit, gate_lanes[:, :, None, :], 0.0), axis=1).astype(BF)
    hit_t = (lanes[:, :, :, None] == row_slot[None, None, None, :]) & own_group.T[None, None]
    plain_t = jnp.sum(hit_t.astype(F32), axis=1).astype(BF)
    gated_t = jnp.sum(jnp.where(hit_t, gate_lanes[:, :, :, None], 0.0), axis=1).astype(BF)
    return plain, gated, plain_t, gated_t


LEG_F0, LEG_B0, LEG_C0, LEG_B1, LEG_F1, LEG_C1 = range(6)
LEGS = 6
RETURNS = 4


def kernel(
    parts,
    hold_a,
    enter_a,
    saved_b,
    hold_g,
    enter_g,
    gain,
    sel,
    comb,
    p1,
    p2,
    wg_hbm,
    wu_hbm,
    wd_hbm,
    made,
    grad,
    wg,
    wu,
    wd,
    xblk,
    sblk,
    cblk,
    nblk,
    inv_b,
    dn,
    perm_f,
    perm_out,
    perm_b,
    zsend,
    zrecv,
    xout,
    xin,
    oute,
    xret,
    zback,
    zret,
    acc,
    acc_c,
    hid,
    w_sem,
    zs_sem,
    zr_sem,
    xs_sem,
    xr_sem,
    ps_sem,
    pr_sem,
):
    n_pipe = lax.axis_size("pipe")
    pipe = lax.axis_index("pipe")
    x, z, c = place_of(lax.axis_index("expert"))
    tokens = hold_a.shape[0]
    width = parts * PART
    blocks = parts * GROUPS

    def along_z(r, sign):
        return (pipe, x * (ZN * 2) + (z + ZN + sign * (r // 2)) % ZN * 2 + (c + r % 2) % 2)

    def along_x(dx, sign):
        return (pipe, (x + XN + sign * dx) % XN * (ZN * 2) + z * 2 + c)

    def along_pipe(sign):
        return ((pipe + n_pipe + sign) % n_pipe, lax.axis_index("expert"))

    weights = [
        pltpu.make_async_copy(wg_hbm, wg, w_sem.at[0]),
        pltpu.make_async_copy(wu_hbm, wu, w_sem.at[1]),
        pltpu.make_async_copy(wd_hbm, wd, w_sem.at[2]),
    ]
    for copy in weights:
        copy.start()

    barrier = pltpu.get_barrier_semaphore()
    greeted = [along_z(r, 1) for r in range(1, PEERS)]
    greeted += [along_x(dx, 1) for dx in range(1, XN)]
    greeted += [along_pipe(1), along_pipe(-1)]
    for peer in greeted:
        pl.semaphore_signal(barrier, inc=1, device_id=peer, device_id_type=MESH)

    def to_blocks(rows, ref, tick):
        for b in range(blocks):
            ref[tick, b] = rows[:, b * COL : (b + 1) * COL]

    def norm_blocks(ref, tick, leg):
        as_float = ref[tick].astype(F32)
        square = jnp.sum(jnp.sum(as_float * as_float, axis=0), axis=1, keepdims=True)
        inverse = lax.rsqrt(square * (1.0 / width) + epsilon)
        for b in range(blocks):
            gain_row = gain[:, b * COL : (b + 1) * COL].astype(F32)
            nblk[leg, b] = (as_float[b] * inverse * gain_row).astype(BF)
        return inverse

    to_blocks(hold_a[...], xblk, 0)
    norm_blocks(xblk, 0, LEG_F0)
    pl.semaphore_wait(barrier, len(greeted))

    def send(src, dst, s_sem, r_sem, peer):
        pltpu.make_async_remote_copy(
            src_ref=src,
            dst_ref=dst,
            send_sem=s_sem,
            recv_sem=r_sem,
            device_id=peer,
            device_id_type=MESH,
        ).start()

    def wait_for(ref, sem):
        pltpu.make_async_copy(ref, ref, sem).wait()

    def between(s, low, high):
        return (s >= low) & (s < high)

    def select(leg, n):
        rows = nblk[leg, pl.ds(n * GROUPS, GROUPS)].reshape(GROUPS * tokens, COL)
        picked = jnp.dot(sel[leg], rows, preferred_element_type=F32).astype(BF)
        picked = picked.reshape(PEERS, SLOTS, COL)
        zrecv[leg, n, 0] = picked[0]
        zsend[leg, n] = picked
        for r in (4, 5, 2, 3, 6, 7, 1):
            send(
                zsend.at[leg, n, r],
                zrecv.at[leg, n, r],
                zs_sem.at[leg],
                zr_sem.at[leg, n],
                along_z(r, 1),
            )

    def spread(leg, n):
        wait_for(zrecv.at[leg, n, pl.ds(1, PEERS - 1)], zr_sem.at[leg, n])
        rows = zrecv[leg, n].reshape(PEERS * SLOTS, COL)
        sorted_rows = jnp.dot(p1[...], rows, preferred_element_type=F32).astype(BF)
        sorted_rows = sorted_rows.reshape(GROUPS, 2, SLOTS, COL)
        for q in (1, 0):
            for g in range(GROUPS):
                xout[leg, n, q, :, g * COL : (g + 1) * COL] = sorted_rows[g, q]
                if q == 0:
                    xin[leg, n, 0, :, g * COL : (g + 1) * COL] = sorted_rows[g, q]
        for dx in (2, 1, 3):
            send(
                xout.at[leg, n, dx % 2],
                xin.at[leg, n, dx],
                xs_sem.at[leg],
                xr_sem.at[leg, n],
                along_x(dx, 1),
            )

    def wait_rows(leg, n):
        wait_for(xin.at[leg, n, pl.ds(1, XN - 1)], xr_sem.at[leg, n])
        return xin[leg, n].reshape(XN * SLOTS, PART)

    def expert_in(leg, n, back):
        rows = wait_rows(leg, n)
        for j, w in enumerate((wg, wu)):
            product = jnp.dot(rows, w[n], preferred_element_type=F32)
            acc[back, j] = jnp.where(n == 0, 0.0, acc[back, j]) + product

    def columns(n):
        return pl.ds(pl.multiple_of(n * PART, PART), PART)

    contract = (((1,), (1,)), ((), ()))

    def expert_cot(leg, n):
        rows = wait_rows(leg, n)
        product = lax.dot_general(rows, wd[:, columns(n)], contract, preferred_element_type=F32)
        acc_c[...] = jnp.where(n == 0, 0.0, acc_c[...]) + product

    def give_back(leg, n, piece):
        piece = piece.astype(BF).reshape(XN, SLOTS, PART)
        xret[leg, n, 0] = piece[0]
        oute[leg, n] = piece
        for dx in (2, 1, 3):
            send(
                oute.at[leg, n, dx],
                xret.at[leg, n, dx],
                xs_sem.at[LEGS + leg],
                xr_sem.at[LEGS + leg, n],
                along_x(dx, -1),
            )

    def out_forward(leg, n):
        give_back(leg, n, jnp.dot(hid[0], wd[:, columns(n)], preferred_element_type=F32))

    def out_backward(leg, n):
        piece = lax.dot_general(hid[1], wg[n], contract, preferred_element_type=F32)
        piece += lax.dot_general(hid[2], wu[n], contract, preferred_element_type=F32)
        give_back(leg, n, piece)

    def gather_back(leg, n):
        wait_for(xret.at[leg, n, pl.ds(1, XN - 1)], xr_sem.at[LEGS + leg, n])
        rows = xret[leg, n].reshape(XN * SLOTS, PART)
        stacked = jnp.concatenate(
            [rows[:, g * COL : (g + 1) * COL] for g in range(GROUPS)], axis=0
        )
        sums = jnp.dot(p2[...], stacked, preferred_element_type=F32).astype(BF)
        sums = sums.reshape(PEERS, SLOTS, COL)
        zret[leg, n, 0] = sums[0]
        zback[leg, n] = sums
        for r in (4, 5, 2, 3, 6, 7, 1):
            send(
                zback.at[leg, n, r],
                zret.at[leg, n, r],
                zs_sem.at[LEGS + leg],
                zr_sem.at[LEGS + leg, n],
                along_z(r, -1),
            )

    def combine(leg, n):
        wait_for(zret.at[leg, n, pl.ds(1, PEERS - 1)], zr_sem.at[LEGS + leg, n])
        rows = zret[leg, n].reshape(PEERS * SLOTS, COL)
        total = jnp.dot(comb[leg], rows, preferred_element_type=F32)
        return total.reshape(GROUPS, tokens, COL)

    def combine_forward(tick, n):
        total = combine(2 * tick, n)
        result = (xblk[tick, pl.ds(n * GROUPS, GROUPS)].astype(F32) + total).astype(BF)
        xnew = pl.ds(n * GROUPS, GROUPS)
        for g in range(GROUPS):
            start = pl.multiple_of(n * PART + g * COL, COL)
            made[tick, :, pl.ds(start, COL)] = result[g]

        @pl.when(tick == 0)
        def _():
            perm_out[0, xnew] = result
            send(
                perm_out.at[0, xnew],
                perm_f.at[xnew],
                ps_sem.at[0],
                pr_sem.at[0],
                along_pipe(1),
            )

    def combine_backward(tick, n):
        dn[pl.ds(n * GROUPS, GROUPS)] = combine(2 * tick + 1, n)

    def hidden():
        gate_pre, up_pre = acc[0, 0], acc[0, 1]
        hid[0] = (gate_pre * jax.nn.sigmoid(gate_pre) * up_pre).astype(BF)

    def gradients():
        gate_pre, up_pre, grad_hidden = acc[1, 0], acc[1, 1], acc_c[...]
        sigma = jax.nn.sigmoid(gate_pre)
        hid[1] = (grad_hidden * up_pre * sigma * (1.0 + gate_pre * (1.0 - sigma))).astype(BF)
        hid[2] = (grad_hidden * gate_pre * sigma).astype(BF)

    def finish_backward(tick):
        inverse = inv_b[tick][:, :1]
        inner = jnp.zeros((tokens, COL), F32)
        for b in range(blocks):
            gain_row = gain[:, b * COL : (b + 1) * COL].astype(F32)
            inner += sblk[tick, b].astype(F32) * (gain_row * dn[b])
        inner = jnp.sum(inner, axis=1, keepdims=True) * (1.0 / width)
        factor = inverse * inverse * inverse * inner
        for b in range(blocks):
            gain_row = gain[:, b * COL : (b + 1) * COL].astype(F32)
            result = cblk[tick, b].astype(F32) + inverse * (gain_row * dn[b])
            result = (result - sblk[tick, b].astype(F32) * factor).astype(BF)
            grad[tick, :, b * COL : (b + 1) * COL] = result
            perm_out[1, b] = result

        @pl.when(tick == 0)
        def _():
            send(perm_out.at[1], perm_b, ps_sem.at[1], pr_sem.at[1], along_pipe(-1))

    def step(s, carry):
        slot = s // parts

        @pl.when(s == 3)
        def _():
            for tick in range(TICKS):
                to_blocks(saved_b[tick], sblk, tick)
                leg = (LEG_B0, LEG_B1)[tick]
                inverse = norm_blocks(sblk, tick, leg)
                inv_b[tick] = jnp.broadcast_to(inverse, (tokens, COL))
            rows = hold_g[...]
            to_blocks(rows, cblk, 0)
            nblk[LEG_C0] = cblk[0]

        @pl.when(s == 4)
        def _():
            for copy in weights:
                copy.wait()

        @pl.when((s == 11) | (s == 53))
        def _():
            hidden()

        @pl.when((s == 25) | (s == 60))
        def _():
            gradients()

        @pl.when(s == 42)
        def _():
            wait_for(perm_f, pr_sem.at[0])
            to_blocks(enter_a[...], xblk, 1)
            xblk[1] = jnp.where(pipe == 0, xblk[1], perm_f[...])
            norm_blocks(xblk, 1, LEG_F1)

        @pl.when((s == 44) | (s == 76))
        def _():
            finish_backward(s // 76)

        @pl.when(s == 49)
        def _():
            wait_for(perm_b, pr_sem.at[1])
            wait_for(perm_out.at[1], ps_sem.at[1])
            to_blocks(enter_g[...], cblk, 1)
            cblk[1] = jnp.where(pipe == n_pipe - 1, cblk[1], perm_b[...])
            nblk[LEG_C1] = cblk[1]

        @pl.when(between(s, 2, 23) | between(s, 37, 58))
        def _():
            turn = (s - 2) // parts
            spread(jnp.where(turn < 3, turn, turn - 2), (s - 2) % parts)

        @pl.when(between(s, 23, 30) | between(s, 58, 65))
        def _():
            out_forward((s // 58) * 2, (s - 23) % parts)

        @pl.when(between(s, 30, 37) | between(s, 65, 72))
        def _():
            out_backward((s // 65) * 2 + 1, (s - 23) % parts)

        @pl.when(between(s, 28, 42))
        def _():
            gather_back((s - 28) // parts, (s - 28) % parts)

        @pl.when(between(s, 60, 74))
        def _():
            gather_back((s - 60) // parts + 2, (s - 60) % parts)

        @pl.when(between(s, 0, 28) | between(s, 42, 56))
        def _():
            select(jnp.where(slot < 4, slot, slot - 2), s % parts)

        @pl.when(between(s, 30, 37) | between(s, 62, 69))
        def _():
            combine_forward(s // 62, (s - 30 - (s // 62) * 32) % parts)

        @pl.when(between(s, 37, 44) | between(s, 69, 76))
        def _():
            combine_backward(s // 69, (s - 37 - (s // 69) * 32) % parts)

        @pl.when(between(s, 4, 18) | between(s, 39, 53))
        def _():
            turn = (s - 4) // parts
            leg = jnp.where(turn < 2, turn, turn - 2)
            expert_in(leg, (s - 4) % parts, leg % 2)

        @pl.when(between(s, 18, 25) | between(s, 53, 60))
        def _():
            turn = (s - 4) // parts
            expert_cot(jnp.where(turn < 3, turn, turn - 2), (s - 4) % parts)

        return carry

    lax.fori_loop(0, 77, step, 0)

    for leg in range(LEGS):
        wait_for(zsend.at[leg, :, pl.ds(1, PEERS - 1)], zs_sem.at[leg])
        wait_for(xin.at[leg, :, pl.ds(1, XN - 1)], xs_sem.at[leg])
    for leg in range(RETURNS):
        wait_for(zback.at[leg, :, pl.ds(1, PEERS - 1)], zs_sem.at[LEGS + leg])
        wait_for(oute.at[leg, :, pl.ds(1, XN - 1)], xs_sem.at[LEGS + leg])
    wait_for(perm_out.at[0], ps_sem.at[0])


def body(
    hold_a,
    enter_a,
    saved_b,
    hold_g,
    enter_g,
    gain,
    w_gate,
    w_up,
    w_down,
    route_a,
    gate_a,
    route_b,
    gate_b,
):
    tokens, width = enter_a.shape
    hidden_units = w_down.shape[1]
    parts = width // PART
    blocks = parts * GROUPS
    route = jnp.concatenate([route_a[:, 0], route_b[:, 0]], axis=0)
    gate = jnp.concatenate([gate_a[:, 0], gate_b[:, 0]], axis=0)
    plain, gated, plain_t, gated_t = route_tables(route, gate)
    sel = jnp.stack([plain[0], plain[2], gated[2], plain[3], plain[1], gated[3]])
    comb = jnp.stack([gated_t[0], plain_t[2], gated_t[1], plain_t[3]])
    p1, p2 = perm_tables()
    vmem = pl.BlockSpec(memory_space=pltpu.VMEM)
    hbm = pl.BlockSpec(memory_space=pl.ANY)
    rows = XN * SLOTS
    out = jax.ShapeDtypeStruct((TICKS, tokens, width), BF)
    token_blocks = (blocks, tokens, COL)
    z_block = (parts, PEERS, SLOTS, COL)
    made, grad = pl.pallas_call(
        functools.partial(kernel, parts),
        out_shape=(out, out),
        in_specs=[vmem] * 10 + [hbm] * 3,
        out_specs=(vmem, vmem),
        scratch_shapes=[
            pltpu.VMEM((parts, PART, hidden_units), BF),
            pltpu.VMEM((parts, PART, hidden_units), BF),
            pltpu.VMEM((hidden_units, width), BF),
            pltpu.VMEM((TICKS,) + token_blocks, BF),
            pltpu.VMEM((TICKS,) + token_blocks, BF),
            pltpu.VMEM((TICKS,) + token_blocks, BF),
            pltpu.VMEM((LEGS,) + token_blocks, BF),
            pltpu.VMEM((TICKS, tokens, COL), F32),
            pltpu.VMEM(token_blocks, F32),
            pltpu.VMEM(token_blocks, BF),
            pltpu.VMEM((2,) + token_blocks, BF),
            pltpu.VMEM(token_blocks, BF),
            pltpu.VMEM((LEGS,) + z_block, BF),
            pltpu.VMEM((LEGS,) + z_block, BF),
            pltpu.VMEM((LEGS, parts, 2, SLOTS, PART), BF),
            pltpu.VMEM((LEGS, parts, XN, SLOTS, PART), BF),
            pltpu.VMEM((RETURNS, parts, XN, SLOTS, PART), BF),
            pltpu.VMEM((RETURNS, parts, XN, SLOTS, PART), BF),
            pltpu.VMEM((RETURNS,) + z_block, BF),
            pltpu.VMEM((RETURNS,) + z_block, BF),
            pltpu.VMEM((2, 2, rows, hidden_units), F32),
            pltpu.VMEM((rows, hidden_units), F32),
            pltpu.VMEM((3, rows, hidden_units), BF),
            pltpu.SemaphoreType.DMA((3,)),
            pltpu.SemaphoreType.DMA((LEGS + RETURNS,)),
            pltpu.SemaphoreType.DMA((LEGS + RETURNS, parts)),
            pltpu.SemaphoreType.DMA((LEGS + RETURNS,)),
            pltpu.SemaphoreType.DMA((LEGS + RETURNS, parts)),
            pltpu.SemaphoreType.DMA((2,)),
            pltpu.SemaphoreType.DMA((2,)),
        ],
        compiler_params=pltpu.CompilerParams(
            collective_id=0, has_side_effects=True, vmem_limit_bytes=62 * 2**20
        ),
        name="relay",
    )(
        hold_a[0],
        enter_a,
        saved_b[:, 0],
        hold_g[0],
        enter_g,
        gain,
        sel,
        comb,
        jnp.asarray(p1, BF),
        jnp.asarray(p2, BF),
        w_gate[0].reshape(parts, PART, hidden_units),
        w_up[0].reshape(parts, PART, hidden_units),
        w_down[0],
    )
    return (made[:, None], grad[:, None])


def solution(mesh):
    placed = (
        P("pipe", "expert", None),
        P("expert", None),
        P(None, "pipe", "expert", None),
        P("pipe", "expert", None),
        P("expert", None),
        P("pipe", None),
        P("pipe", None, "expert"),
        P("pipe", None, "expert"),
        P("pipe", "expert", None),
        P(None, "pipe", "expert", None),
        P(None, "pipe", "expert", None),
        P(None, "pipe", "expert", None),
        P(None, "pipe", "expert", None),
    )
    return jax.shard_map(
        body,
        mesh=mesh,
        in_specs=placed,
        out_specs=(P(None, "pipe", "expert", None), P(None, "pipe", "expert", None)),
        check_vma=False,
    )
```

time: 553 us -> 225 us (0.41); the launches traced: 543 us -> 224 us
  waiting for transfers between devices: 313 us -> 0 us
  Pallas kernels: 0 us -> 212 us
  starting transfers between devices: 93.4 us -> 0 us
  matrix products: 64.8 us -> 0 us
  local copies, waits for them, and re-layouts: 58.5 us -> 5.93 us
  other arithmetic: 11.9 us -> 5.22 us
    all_to_all x10 -> x0, waiting for transfers between devices: 301 us -> none  [the longest x4 121 us: run_experts(): lax.all_to_all(buffers[0], 'expert', split_axis=0, concat_axis=0, tiled=T...]
    pallas_call x0 -> x1, Pallas kernels: none -> 212 us  [body(): pl.pallas_call(functools.partial(kernel, parts), out_shape=(out, out), in...]
    all_to_all x10 -> x0, starting transfers between devices: 90.7 us -> none  [the longest x4 34.3 us: run_experts(): lax.all_to_all(partial_value, 'expert', split_axis=0, concat_axis=0, tile...]
    dot_general x22 -> x0, matrix products: 64.8 us -> none  [the longest x2 13.9 us: backward_kernel(): lax.dot_general(grad_gate, weights[0], contract, preferred_element_type=j...]
    reshape x20 -> x0, local copies, waits for them, and re-layouts: 36.6 us -> none  [the longest x6 13.8 us: run_experts(): item.reshape(devices * capacity, feature_count)]
    ppermute x2 -> x0, waiting for transfers between devices: 11.8 us -> none  [from_behind(): return lax.ppermute(block, axis, route)]
    convert_element_type x4 -> x0, local copies, waits for them, and re-layouts: 9.59 us -> none  [run_experts(): returned.reshape(slices, experts * capacity, feature_count)]
  transfers between devices with their start and end apart: 12 -> 0, of which waited for: 12 -> 0; matrix products, arithmetic and copies ran while one was open for 21% -> 0% of each run, Pallas kernels for 0% -> 0%
where the time goes in v1:
time: 225 us; the launch traced here: 224 us
  Pallas kernels  212 us (94%)
  local copies, waits for them, and re-layouts  5.93 us (3%)
  other arithmetic  5.22 us (2%)
    pallas_call x1, Pallas kernels, body(): pl.pallas_call(functools.partial(kernel, parts), out_shape=(out, out), in...  212 us
    unnamed x14, local copies, waits for them, and re-layouts  5.27 us

profile of v1, /device:TPU:1, one launch (start us, length us, event | category | flops | bytes accessed | tf_op | source)
XLA Modules:
  0.0 224.3 jit_solution(17963589905969799583)
XLA Ops:
  0.6 0.0 copy-start.1
  0.6 0.7 fusion.4
  1.4 0.1 tile.19
  1.5 0.8 copy.39
  2.2 0.1 concatenate.23
  2.3 0.8 copy.38
  3.1 0.1 concatenate.22
  3.2 0.1 fusion
  3.3 0.1 reduce_window_sum.11
  3.5 0.2 select_reduce_fusion.2
  3.7 0.1 copy.40
  3.8 0.1 copy.41
  3.9 0.7 fusion.2
  4.6 0.1 tile.17
  4.7 0.7 fusion.9
  5.5 1.3 select_reduce_fusion.1
  6.9 0.0 copy-done.1
  6.9 0.0 copy-start
  6.9 0.5 select_reduce_fusion
  7.5 0.8 pad_maximum_fusion.comb
  8.3 0.0 copy-done
  8.3 212.4 %relay.1 = (bf16[2,32,3584]{2,1,0:T(8,128)(2,1)}, bf16[2,32,3584]{2,1,0:T(8,128)(2,1)}) custom-call(bf16[32,3584]{1,0:T(8,128)(2,1)} %bitcast.38, bf16[32,3584]{1,0:T(8,128)(2,1)} %enter_a.1, bf16[2,32,3584]{2,1,0:T(8,128)(2,1)} %bitcast.37, bf16[32,3584]{1,0:T(8,128)(2,1)} %bitcast.39, bf16[32,3584]{1,0:T(8,128)(2,1)} %enter_g.1, bf16[1,3584]{1,0:T(2,128)(2,1)} %gain.1, ...), custom_call_target="tpu_custom_call" | custom-call | tf_op jit(solution)/shard_map/relay/pallas_call | solution.py:478
  220.7 1.8 copy.52
  222.5 1.8 copy.53
  (11 shorter events, 0.2 us)
Async XLA Ops:
  0.6 6.3 %copy-start.1 = (pred[128,384]{1,0:T(32,128)(4,1)S(1)}, pred[128,384]{1,0:T(32,128)(4,1)}, u32[]{:S(2)}) copy-start(pred[128,384]{1,0:T(32,128)(4,1)} %constant.117) | copy-start | bytes 147460
  6.9 1.4 copy-start

commit v2 on v1

v2 whole, which is shorter than its diff:
```python
import functools

import jax
import jax.numpy as jnp
from jax import lax
from jax.experimental import pallas as pl
from jax.experimental.pallas import tpu as pltpu
from jax.sharding import PartitionSpec as P

SLICES = 2
TOP = 2
TICKS = 2
CAP = 6
MESH = pl.DeviceIdType.MESH
BF = jnp.bfloat16
F32 = jnp.float32

epsilon = 1e-06
gate_unit = 1.0 / 256.0

XN = 4
ZN = 4
PEERS = 8
GROUPS = 4
SLOTS = 48
COL = 128
PART = GROUPS * COL
LAG_Z = 3
LAG_X = 2
GROUP_STEP = 1024
VMEM_MIB = 51
SENDING = 3
RETURNING = 2


def place_of(index):
    return index // (ZN * 2), (index // 2) % ZN, index % 2


def fields(row):
    six = (row * 10923) >> 16
    return (row * 21846) >> 20, ((row * 5462) >> 16) & (GROUPS - 1), six & 1, row - six * CAP


LEG_F0, LEG_B0, LEG_C0, LEG_B1, LEG_F1, LEG_C1 = range(6)
LEGS = 6
RETURNS = 4


RET_F0, RET_B0, RET_F1, RET_B1 = range(RETURNS)


def schedule(parts):
    x_order = [
        (LEG_F0, False),
        (LEG_B0, False),
        (LEG_C0, False),
        (RET_F0, True),
        (RET_B0, True),
        (LEG_B1, False),
        (LEG_F1, False),
        (LEG_C1, False),
        (RET_F1, True),
        (RET_B1, True),
    ]
    spread, give = {}, {}
    for turn, (leg, back) in enumerate(x_order):
        (give if back else spread)[leg] = LAG_Z + turn * parts
    arrive = {leg: first + LAG_X for leg, first in spread.items()}
    z_order = [LEG_F0, LEG_B0, LEG_C0, LEG_B1, None, None, LEG_F1, LEG_C1]
    select = {leg: turn * parts for turn, leg in enumerate(z_order) if leg is not None}
    gather, free = {}, 4 * parts
    for leg in range(RETURNS):
        if leg == RET_F1:
            free = 8 * parts
        gather[leg] = max(free, give[leg] + LAG_X)
        free = gather[leg] + parts
    combine = {leg: first + LAG_Z for leg, first in gather.items()}
    plan = {
        "prepare": 4,
        "weights": arrive[LEG_F0],
        "hidden": (arrive[LEG_F0] + parts, arrive[LEG_F1] + parts),
        "gradients": (arrive[LEG_C0] + parts, arrive[LEG_C1] + parts),
        "enter_f": select[LEG_F1],
        "enter_b": select[LEG_C1],
        "finish": (combine[RET_B0] + parts, combine[RET_B1] + parts),
        "spread": [(spread[leg], leg) for leg in range(LEGS)],
        "out_forward": [(give[leg], leg) for leg in (RET_F0, RET_F1)],
        "out_backward": [(give[leg], leg) for leg in (RET_B0, RET_B1)],
        "gather_back": [(gather[leg], leg) for leg in range(RETURNS)],
        "select": [(select[leg], leg) for leg in range(LEGS)],
        "combine_forward": [(combine[leg], leg // 2) for leg in (RET_F0, RET_F1)],
        "combine_backward": [(combine[leg], leg // 2) for leg in (RET_B0, RET_B1)],
        "expert_in": [(arrive[leg], leg) for leg in (LEG_F0, LEG_B0, LEG_B1, LEG_F1)],
        "expert_cot": [(arrive[leg], leg) for leg in (LEG_C0, LEG_C1)],
    }
    return plan


def kernel(
    parts,
    hold_a_hbm,
    enter_a_hbm,
    saved_b_hbm,
    hold_g_hbm,
    enter_g_hbm,
    gain_hbm,
    route_a_hbm,
    gate_a_hbm,
    route_b_hbm,
    gate_b_hbm,
    wg_hbm,
    wu_hbm,
    wd_hbm,
    made,
    grad,
    hold_a,
    enter_a,
    saved_b,
    hold_g,
    enter_g,
    gain,
    route_a,
    gate_a,
    route_b,
    gate_b,
    wg,
    wu,
    wd,
    xblk,
    sblk,
    cblk,
    nblk,
    inv_b,
    dn,
    perm_f,
    perm_out,
    perm_b,
    zsend,
    zrecv,
    xout,
    xin,
    oute,
    xret,
    zback,
    zret,
    acc,
    acc_c,
    hid,
    sel,
    comb,
    p1,
    p2,
    w_sem,
    zs_sem,
    zr_sem,
    xs_sem,
    xr_sem,
    ps_sem,
    pr_sem,
):
    n_pipe = lax.axis_size("pipe")
    pipe = lax.axis_index("pipe")
    x, z, c = place_of(lax.axis_index("expert"))
    tokens = hold_a.shape[0]
    width = parts * PART
    blocks = parts * GROUPS

    def along_z(r, sign):
        return (pipe, x * (ZN * 2) + (z + ZN + sign * (r // 2)) % ZN * 2 + (c + r % 2) % 2)

    def along_x(dx, sign):
        return (pipe, (x + XN + sign * dx) % XN * (ZN * 2) + z * 2 + c)

    def along_pipe(sign):
        return ((pipe + n_pipe + sign) % n_pipe, lax.axis_index("expert"))

    pairs = [
        (hold_a_hbm, hold_a),
        (gain_hbm, gain),
        (route_a_hbm, route_a),
        (gate_a_hbm, gate_a),
        (route_b_hbm, route_b),
        (gate_b_hbm, gate_b),
        (saved_b_hbm, saved_b),
        (hold_g_hbm, hold_g),
        (wg_hbm, wg),
        (wu_hbm, wu),
        (wd_hbm, wd),
        (enter_a_hbm, enter_a),
        (enter_g_hbm, enter_g),
    ]
    loads = [pltpu.make_async_copy(*pair, w_sem.at[i]) for i, pair in enumerate(pairs)]
    for copy in loads:
        copy.start()

    barrier = pltpu.get_barrier_semaphore()
    greeted = [along_z(r, 1) for r in range(1, PEERS)]
    greeted += [along_x(dx, 1) for dx in range(1, XN)]
    greeted += [along_pipe(1), along_pipe(-1)]
    for peer in greeted:
        pl.semaphore_signal(barrier, inc=1, device_id=peer, device_id_type=MESH)

    def to_blocks(rows, ref, tick):
        for b in range(blocks):
            ref[tick, b] = rows[:, b * COL : (b + 1) * COL]

    def norm_blocks(ref, tick, leg):
        as_float = ref[tick].astype(F32)
        square = jnp.sum(jnp.sum(as_float * as_float, axis=0), axis=1, keepdims=True)
        inverse = lax.rsqrt(square * (1.0 / width) + epsilon)
        for b in range(blocks):
            gain_row = gain[:, b * COL : (b + 1) * COL].astype(F32)
            nblk[leg, b] = (as_float[b] * inverse * gain_row).astype(BF)
        return inverse

    def slot_of_row(row):
        r, group, q, slot = fields(row)
        expert = ((x + q) & 1) * (ZN * 2) + ((z + (r >> 1)) & (ZN - 1)) * 2 + ((c + r) & 1)
        return expert * CAP + slot + group * GROUP_STEP

    def make_p1():
        shape = (PEERS * SLOTS, PEERS * SLOTS)
        r, group, q, slot = fields(lax.broadcasted_iota(jnp.int32, (1, shape[1]), 1))
        target = (group * 2 + q) * SLOTS + r * CAP + slot
        hit = lax.broadcasted_iota(jnp.int32, shape, 0) == target
        p1[...] = jnp.where(hit, 1.0, 0.0).astype(BF)

    def make_p2():
        shape = (PEERS * SLOTS, GROUPS * XN * SLOTS)
        column = lax.broadcasted_iota(jnp.int32, (1, shape[1]), 1)
        block = (column * 21846) >> 20
        six = (column * 10923) >> 16
        target = (six & (PEERS - 1)) * SLOTS + (block >> 2) * 2 * CAP
        target += (block & 1) * CAP + column - six * CAP
        hit = lax.broadcasted_iota(jnp.int32, shape, 0) == target
        p2[...] = jnp.where(hit, 1.0, 0.0).astype(BF)

    def route_tables(route, gate, plain_to, gated_to, back_to, gate_back):
        row = [route[k : k + 1] for k in range(TOP)]
        token = lax.broadcasted_iota(jnp.int32, (tokens, tokens), 0)
        other = lax.broadcasted_iota(jnp.int32, (tokens, tokens), 1)
        col = [jnp.sum(jnp.where(token == other, v, 0), axis=1, keepdims=True) for v in row]
        slots = []
        for k in range(TOP):
            same = jnp.where((col[k] == row[k]) & (other < token), 1, 0)
            for j in range(k):
                same += jnp.where(col[k] == row[j], 1, 0)
            slots.append(col[k] * CAP + jnp.sum(same, axis=1, keepdims=True))
        shape = (GROUPS * tokens, GROUPS * tokens)
        down = lax.broadcasted_iota(jnp.int32, shape, 0)
        eye = down == lax.broadcasted_iota(jnp.int32, shape, 1)
        id_col, id_row, g_col, g_row = [], [], [], []
        for k in range(TOP):
            ids = [slots[k] + g * GROUP_STEP for g in range(GROUPS)]
            ids = jnp.concatenate(ids, axis=0)
            value = jnp.where(token == other, gate[k : k + 1], 0)
            value = jnp.sum(value, axis=1, keepdims=True).astype(F32) * gate_unit
            value = jnp.concatenate([value] * GROUPS, axis=0)
            id_col.append(ids)
            g_col.append(value)
            id_row.append(jnp.sum(jnp.where(eye, ids, 0), axis=0, keepdims=True))
            g_row.append(jnp.sum(jnp.where(eye, value, 0.0), axis=0, keepdims=True))
        own = slot_of_row(lax.broadcasted_iota(jnp.int32, (PEERS * SLOTS, 1), 0))
        hits = [own == v for v in id_row]
        if plain_to is not None:
            sel[plain_to] = jnp.where(hits[0] | hits[1], 1.0, 0.0).astype(BF)
        if gated_to is not None:
            gated = jnp.where(hits[0], g_row[0], jnp.where(hits[1], g_row[1], 0.0))
            sel[gated_to] = gated.astype(BF)
        own = slot_of_row(lax.broadcasted_iota(jnp.int32, (1, PEERS * SLOTS), 1))
        hits = [own == v for v in id_col]
        if gate_back:
            back = jnp.where(hits[0], g_col[0], jnp.where(hits[1], g_col[1], 0.0))
        else:
            back = jnp.where(hits[0] | hits[1], 1.0, 0.0)
        comb[back_to] = back.astype(BF)

    for copy in loads[:4]:
        copy.wait()
    to_blocks(hold_a[...], xblk, 0)
    norm_blocks(xblk, 0, LEG_F0)
    route_tables(route_a[0], gate_a[0], LEG_F0, None, RET_F0, True)
    pl.semaphore_wait(barrier, len(greeted))

    def send(src, dst, s_sem, r_sem, peer):
        pltpu.make_async_remote_copy(
            src_ref=src,
            dst_ref=dst,
            send_sem=s_sem,
            recv_sem=r_sem,
            device_id=peer,
            device_id_type=MESH,
        ).start()

    def wait_for(ref, sem):
        pltpu.make_async_copy(ref, ref, sem).wait()

    def between(s, low, high):
        return (s >= low) & (s < high)

    def select(leg, n):
        rows = nblk[leg, pl.ds(n * GROUPS, GROUPS)].reshape(GROUPS * tokens, COL)
        picked = jnp.dot(sel[leg], rows, preferred_element_type=F32).astype(BF)
        picked = picked.reshape(PEERS, SLOTS, COL)
        turn = lax.rem(leg, SENDING)

        @pl.when((leg >= SENDING) & (n == 0))
        def _():
            wait_for(zsend.at[turn, :, pl.ds(1, PEERS - 1)], zs_sem.at[leg - SENDING])

        zrecv[leg, n, 0] = picked[0]
        zsend[turn, n] = picked
        for r in (4, 5, 2, 3, 6, 7, 1):
            send(
                zsend.at[turn, n, r],
                zrecv.at[leg, n, r],
                zs_sem.at[leg],
                zr_sem.at[leg, n],
                along_z(r, 1),
            )

    def spread(leg, n):
        wait_for(zrecv.at[leg, n, pl.ds(1, PEERS - 1)], zr_sem.at[leg, n])
        rows = zrecv[leg, n].reshape(PEERS * SLOTS, COL)
        sorted_rows = jnp.dot(p1[...], rows, preferred_element_type=F32).astype(BF)
        sorted_rows = sorted_rows.reshape(GROUPS, 2, SLOTS, COL)
        turn = lax.rem(leg, SENDING)

        @pl.when((leg >= SENDING) & (n == 0))
        def _():
            wait_for(xin.at[leg, :, pl.ds(1, XN - 1)], xs_sem.at[leg - SENDING])

        for q in (1, 0):
            for g in range(GROUPS):
                xout[turn, n, q, :, g * COL : (g + 1) * COL] = sorted_rows[g, q]
                if q == 0:
                    xin[leg, n, 0, :, g * COL : (g + 1) * COL] = sorted_rows[g, q]
        for dx in (2, 1, 3):
            send(
                xout.at[turn, n, dx % 2],
                xin.at[leg, n, dx],
                xs_sem.at[leg],
                xr_sem.at[leg, n],
                along_x(dx, 1),
            )

    def wait_rows(leg, n):
        wait_for(xin.at[leg, n, pl.ds(1, XN - 1)], xr_sem.at[leg, n])
        return xin[leg, n].reshape(XN * SLOTS, PART)

    def expert_in(leg, n):
        rows = wait_rows(leg, n)
        back = lax.rem(leg, 2)
        for j, w in enumerate((wg, wu)):
            product = jnp.dot(rows, w[n], preferred_element_type=F32)
            acc[back, j] = jnp.where(n == 0, 0.0, acc[back, j]) + product

    def columns(n):
        return pl.ds(pl.multiple_of(n * PART, PART), PART)

    contract = (((1,), (1,)), ((), ()))

    def expert_cot(leg, n):
        rows = wait_rows(leg, n)
        product = lax.dot_general(rows, wd[:, columns(n)], contract, preferred_element_type=F32)
        acc_c[...] = jnp.where(n == 0, 0.0, acc_c[...]) + product

    def give_back(leg, n, piece):
        piece = piece.astype(BF).reshape(XN, SLOTS, PART)
        turn = lax.rem(leg, RETURNING)

        @pl.when((leg >= RETURNING) & (n == 0))
        def _():
            wait_for(oute.at[turn, :, pl.ds(1, XN - 1)], xs_sem.at[LEGS + leg - RETURNING])

        xret[leg, n, 0] = piece[0]
        oute[turn, n] = piece
        for dx in (2, 1, 3):
            send(
                oute.at[turn, n, dx],
                xret.at[leg, n, dx],
                xs_sem.at[LEGS + leg],
                xr_sem.at[LEGS + leg, n],
                along_x(dx, -1),
            )

    def out_forward(leg, n):
        give_back(leg, n, jnp.dot(hid[0], wd[:, columns(n)], preferred_element_type=F32))

    def out_backward(leg, n):
        piece = lax.dot_general(hid[1], wg[n], contract, preferred_element_type=F32)
        piece += lax.dot_general(hid[2], wu[n], contract, preferred_element_type=F32)
        give_back(leg, n, piece)

    def gather_back(leg, n):
        wait_for(xret.at[leg, n, pl.ds(1, XN - 1)], xr_sem.at[LEGS + leg, n])
        rows = xret[leg, n].reshape(XN * SLOTS, PART)
        stacked = jnp.concatenate(
            [rows[:, g * COL : (g + 1) * COL] for g in range(GROUPS)], axis=0
        )
        sums = jnp.dot(p2[...], stacked, preferred_element_type=F32).astype(BF)
        sums = sums.reshape(PEERS, SLOTS, COL)
        turn = lax.rem(leg, RETURNING)

        @pl.when((leg >= RETURNING) & (n == 0))
        def _():
            wait_for(zback.at[turn, :, pl.ds(1, PEERS - 1)], zs_sem.at[LEGS + leg - RETURNING])

        zret[leg, n, 0] = sums[0]
        zback[turn, n] = sums
        for r in (4, 5, 2, 3, 6, 7, 1):
            send(
                zback.at[turn, n, r],
                zret.at[leg, n, r],
                zs_sem.at[LEGS + leg],
                zr_sem.at[LEGS + leg, n],
                along_z(r, -1),
            )

    def combine(leg, n):
        wait_for(zret.at[leg, n, pl.ds(1, PEERS - 1)], zr_sem.at[LEGS + leg, n])
        rows = zret[leg, n].reshape(PEERS * SLOTS, COL)
        total = jnp.dot(comb[leg], rows, preferred_element_type=F32)
        return total.reshape(GROUPS, tokens, COL)

    def combine_forward(tick, n):
        total = combine(2 * tick, n)
        result = (xblk[tick, pl.ds(n * GROUPS, GROUPS)].astype(F32) + total).astype(BF)
        xnew = pl.ds(n * GROUPS, GROUPS)
        for g in range(GROUPS):
            start = pl.multiple_of(n * PART + g * COL, COL)
            made[tick, :, pl.ds(start, COL)] = result[g]

        @pl.when(tick == 0)
        def _():
            perm_out[0, xnew] = result
            send(
                perm_out.at[0, xnew],
                perm_f.at[xnew],
                ps_sem.at[0],
                pr_sem.at[0],
                along_pipe(1),
            )

    def combine_backward(tick, n):
        dn[pl.ds(n * GROUPS, GROUPS)] = combine(2 * tick + 1, n)

    def hidden():
        gate_pre, up_pre = acc[0, 0], acc[0, 1]
        hid[0] = (gate_pre * jax.nn.sigmoid(gate_pre) * up_pre).astype(BF)

    def gradients():
        gate_pre, up_pre, grad_hidden = acc[1, 0], acc[1, 1], acc_c[...]
        sigma = jax.nn.sigmoid(gate_pre)
        hid[1] = (grad_hidden * up_pre * sigma * (1.0 + gate_pre * (1.0 - sigma))).astype(BF)
        hid[2] = (grad_hidden * gate_pre * sigma).astype(BF)

    def finish_backward(tick):
        inverse = inv_b[tick][:, :1]
        inner = jnp.zeros((tokens, COL), F32)
        for b in range(blocks):
            gain_row = gain[:, b * COL : (b + 1) * COL].astype(F32)
            inner += sblk[tick, b].astype(F32) * (gain_row * dn[b])
        inner = jnp.sum(inner, axis=1, keepdims=True) * (1.0 / width)
        factor = inverse * inverse * inverse * inner
        for b in range(blocks):
            gain_row = gain[:, b * COL : (b + 1) * COL].astype(F32)
            result = cblk[tick, b].astype(F32) + inverse * (gain_row * dn[b])
            result = (result - sblk[tick, b].astype(F32) * factor).astype(BF)
            grad[tick, :, b * COL : (b + 1) * COL] = result
            perm_out[1, b] = result

        @pl.when(tick == 0)
        def _():
            send(perm_out.at[1], perm_b, ps_sem.at[1], pr_sem.at[1], along_pipe(-1))

    def run(s, runs, task):
        active, leg, start = False, 0, 0
        for first, number in runs:
            active = active | between(s, first, first + parts)
            leg = jnp.where(s >= first, number, leg)
            start = jnp.where(s >= first, first, start)

        @pl.when(active)
        def _():
            task(leg, lax.rem(s - start, parts))

    plan = schedule(parts)

    def step(s, carry):
        @pl.when(s == plan["spread"][0][0] - 1)
        def _():
            make_p1()

        @pl.when(s == plan["prepare"])
        def _():
            for copy in loads[4:8]:
                copy.wait()
            for tick in range(TICKS):
                to_blocks(saved_b[tick], sblk, tick)
                leg = (LEG_B0, LEG_B1)[tick]
                inverse = norm_blocks(sblk, tick, leg)
                inv_b[tick] = jnp.broadcast_to(inverse, (tokens, COL))
                legs = ((LEG_B0, LEG_C0, RET_B0), (LEG_B1, LEG_C1, RET_B1))[tick]
                route_tables(route_b[tick], gate_b[tick], *legs, False)
            to_blocks(hold_g[...], cblk, 0)
            nblk[LEG_C0] = cblk[0]
            route_tables(route_a[1], gate_a[1], LEG_F1, None, RET_F1, True)
            make_p2()

        @pl.when(s == plan["weights"])
        def _():
            for copy in loads[8:]:
                copy.wait()

        @pl.when((s == plan["hidden"][0]) | (s == plan["hidden"][1]))
        def _():
            hidden()

        @pl.when((s == plan["gradients"][0]) | (s == plan["gradients"][1]))
        def _():
            gradients()

        @pl.when(s == plan["enter_f"])
        def _():
            wait_for(perm_f, pr_sem.at[0])
            to_blocks(enter_a[...], xblk, 1)
            xblk[1] = jnp.where(pipe == 0, xblk[1], perm_f[...])
            norm_blocks(xblk, 1, LEG_F1)

        @pl.when((s == plan["finish"][0]) | (s == plan["finish"][1]))
        def _():
            finish_backward(s // plan["finish"][1])

        @pl.when(s == plan["enter_b"])
        def _():
            wait_for(perm_b, pr_sem.at[1])
            wait_for(perm_out.at[1], ps_sem.at[1])
            to_blocks(enter_g[...], cblk, 1)
            cblk[1] = jnp.where(pipe == n_pipe - 1, cblk[1], perm_b[...])
            nblk[LEG_C1] = cblk[1]

        run(s, plan["out_forward"], out_forward)
        run(s, plan["out_backward"], out_backward)
        run(s, plan["select"], select)
        run(s, plan["spread"], spread)
        run(s, plan["gather_back"], gather_back)
        run(s, plan["combine_forward"], combine_forward)
        run(s, plan["combine_backward"], combine_backward)
        run(s, plan["expert_in"], expert_in)
        run(s, plan["expert_cot"], expert_cot)
        return carry

    lax.fori_loop(0, plan["finish"][1] + 1, step, 0)

    for leg in range(LEGS - SENDING, LEGS):
        wait_for(zsend.at[leg % SENDING, :, pl.ds(1, PEERS - 1)], zs_sem.at[leg])
        wait_for(xin.at[leg, :, pl.ds(1, XN - 1)], xs_sem.at[leg])
    for leg in range(RETURNS - RETURNING, RETURNS):
        turn = leg % RETURNING
        wait_for(zback.at[turn, :, pl.ds(1, PEERS - 1)], zs_sem.at[LEGS + leg])
        wait_for(oute.at[turn, :, pl.ds(1, XN - 1)], xs_sem.at[LEGS + leg])
    wait_for(perm_out.at[0], ps_sem.at[0])


def body(
    hold_a,
    enter_a,
    saved_b,
    hold_g,
    enter_g,
    gain,
    w_gate,
    w_up,
    w_down,
    route_a,
    gate_a,
    route_b,
    gate_b,
):
    tokens, width = enter_a.shape
    hidden_units = w_down.shape[1]
    parts = width // PART
    blocks = parts * GROUPS
    route_a, gate_a, route_b, gate_b = (
        v[:, 0].transpose(0, 2, 1) for v in (route_a, gate_a, route_b, gate_b)
    )
    vmem = pl.BlockSpec(memory_space=pltpu.VMEM)
    hbm = pl.BlockSpec(memory_space=pltpu.HBM)
    rows = XN * SLOTS
    out = jax.ShapeDtypeStruct((TICKS, tokens, width), BF)
    token_blocks = (blocks, tokens, COL)
    z_block = (parts, PEERS, SLOTS, COL)
    operands = (
        hold_a[0],
        enter_a,
        saved_b[:, 0],
        hold_g[0],
        enter_g,
        gain,
        route_a,
        gate_a,
        route_b,
        gate_b,
        w_gate[0].reshape(parts, PART, hidden_units),
        w_up[0].reshape(parts, PART, hidden_units),
        w_down[0],
    )
    made, grad = pl.pallas_call(
        functools.partial(kernel, parts),
        out_shape=(out, out),
        in_specs=[hbm] * 13,
        out_specs=(vmem, vmem),
        scratch_shapes=[
            pltpu.VMEM((tokens, width), BF),
            pltpu.VMEM((tokens, width), BF),
            pltpu.VMEM((TICKS, tokens, width), BF),
            pltpu.VMEM((tokens, width), BF),
            pltpu.VMEM((tokens, width), BF),
            pltpu.VMEM((1, width), BF),
            pltpu.VMEM((TICKS, TOP, tokens), jnp.int32),
            pltpu.VMEM((TICKS, TOP, tokens), jnp.int32),
            pltpu.VMEM((TICKS, TOP, tokens), jnp.int32),
            pltpu.VMEM((TICKS, TOP, tokens), jnp.int32),
            pltpu.VMEM((parts, PART, hidden_units), BF),
            pltpu.VMEM((parts, PART, hidden_units), BF),
            pltpu.VMEM((hidden_units, width), BF),
            pltpu.VMEM((TICKS,) + token_blocks, BF),
            pltpu.VMEM((TICKS,) + token_blocks, BF),
            pltpu.VMEM((TICKS,) + token_blocks, BF),
            pltpu.VMEM((LEGS,) + token_blocks, BF),
            pltpu.VMEM((TICKS, tokens, COL), F32),
            pltpu.VMEM(token_blocks, F32),
            pltpu.VMEM(token_blocks, BF),
            pltpu.VMEM((2,) + token_blocks, BF),
            pltpu.VMEM(token_blocks, BF),
            pltpu.VMEM((SENDING,) + z_block, BF),
            pltpu.VMEM((LEGS,) + z_block, BF),
            pltpu.VMEM((SENDING, parts, 2, SLOTS, PART), BF),
            pltpu.VMEM((LEGS, parts, XN, SLOTS, PART), BF),
            pltpu.VMEM((RETURNING, parts, XN, SLOTS, PART), BF),
            pltpu.VMEM((RETURNS, parts, XN, SLOTS, PART), BF),
            pltpu.VMEM((RETURNING,) + z_block, BF),
            pltpu.VMEM((RETURNS,) + z_block, BF),
            pltpu.VMEM((2, 2, rows, hidden_units), F32),
            pltpu.VMEM((rows, hidden_units), F32),
            pltpu.VMEM((3, rows, hidden_units), BF),
            pltpu.VMEM((LEGS, PEERS * SLOTS, GROUPS * tokens), BF),
            pltpu.VMEM((RETURNS, GROUPS * tokens, PEERS * SLOTS), BF),
            pltpu.VMEM((PEERS * SLOTS, PEERS * SLOTS), BF),
            pltpu.VMEM((PEERS * SLOTS, GROUPS * XN * SLOTS), BF),
            pltpu.SemaphoreType.DMA((13,)),
            pltpu.SemaphoreType.DMA((LEGS + RETURNS,)),
            pltpu.SemaphoreType.DMA((LEGS + RETURNS, parts)),
            pltpu.SemaphoreType.DMA((LEGS + RETURNS,)),
            pltpu.SemaphoreType.DMA((LEGS + RETURNS, parts)),
            pltpu.SemaphoreType.DMA((2,)),
            pltpu.SemaphoreType.DMA((2,)),
        ],
        compiler_params=pltpu.CompilerParams(
            collective_id=0, has_side_effects=True, vmem_limit_bytes=VMEM_MIB * 2**20
        ),
        name="relay",
    )(*[pltpu.with_memory_space_constraint(v, pltpu.HBM) for v in operands])
    return (made[:, None], grad[:, None])


def solution(mesh):
    placed = (
        P("pipe", "expert", None),
        P("expert", None),
        P(None, "pipe", "expert", None),
        P("pipe", "expert", None),
        P("expert", None),
        P("pipe", None),
        P("pipe", None, "expert"),
        P("pipe", None, "expert"),
        P("pipe", "expert", None),
        P(None, "pipe", "expert", None),
        P(None, "pipe", "expert", None),
        P(None, "pipe", "expert", None),
        P(None, "pipe", "expert", None),
    )
    return jax.shard_map(
        body,
        mesh=mesh,
        in_specs=placed,
        out_specs=(P(None, "pipe", "expert", None), P(None, "pipe", "expert", None)),
        check_vma=False,
    )
```

time: 225 us -> 187 us (0.83)
  Pallas kernels: 212 us -> 185 us
  other arithmetic: 5.22 us -> 0 us
  local copies, waits for them, and re-layouts: 5.93 us -> 1.54 us
    pallas_call x1, Pallas kernels: 212 us -> 185 us  [body(): pl.pallas_call(functools.partial(kernel, parts), out_shape=(out, out), in...]
    unnamed x14 -> x2, local copies, waits for them, and re-layouts: 5.27 us -> 1.54 us
where the time goes in v2:
time: 187 us
  Pallas kernels  185 us (99%)
    pallas_call x1, Pallas kernels, body(): pl.pallas_call(functools.partial(kernel, parts), out_shape=(out, out), in...  185 us

profile of v2, /device:TPU:1, one launch (start us, length us, event | category | flops | bytes accessed | tf_op | source)
XLA Modules:
  0.0 187.3 jit_solution(12034621542047298796)
XLA Ops:
  0.6 185.2 %relay.1 = (bf16[2,32,3584]{2,1,0:T(8,128)(2,1)S(1)}, bf16[2,32,3584]{2,1,0:T(8,128)(2,1)S(1)}) custom-call(bf16[32,3584]{1,0:T(8,128)(2,1)} %bitcast.30, bf16[32,3584]{1,0:T(8,128)(2,1)} %enter_a_hbm.1, bf16[2,32,3584]{2,1,0:T(8,128)(2,1)} %bitcast.29, bf16[32,3584]{1,0:T(8,128)(2,1)} %bitcast.31, bf16[32,3584]{1,0:T(8,128)(2,1)} %enter_g_hbm.1, ...), custom_call_target="tpu_custom_call" | custom-call | tf_op jit(solution)/shard_map/relay/pallas_call | solution.py:610
  185.8 0.8 copy.19
  186.6 0.8 copy.20

commit v3 on v2

--- a/solution.py
+++ b/solution.py
@@ -112,8 +112,7 @@
     wg_hbm,
     wu_hbm,
     wd_hbm,
-    made,
-    grad,
+    results,
     hold_a,
     enter_a,
     saved_b,
@@ -336,7 +335,7 @@
                 xout[turn, n, q, :, g * COL : (g + 1) * COL] = sorted_rows[g, q]
                 if q == 0:
                     xin[leg, n, 0, :, g * COL : (g + 1) * COL] = sorted_rows[g, q]
-        for dx in (2, 1, 3):
+        for dx in (1, 3, 2):
             send(
                 xout.at[turn, n, dx % 2],
                 xin.at[leg, n, dx],
@@ -376,7 +375,7 @@
 
         xret[leg, n, 0] = piece[0]
         oute[turn, n] = piece
-        for dx in (2, 1, 3):
+        for dx in (1, 3, 2):
             send(
                 oute.at[turn, n, dx],
                 xret.at[leg, n, dx],
@@ -430,7 +429,7 @@
         xnew = pl.ds(n * GROUPS, GROUPS)
         for g in range(GROUPS):
             start = pl.multiple_of(n * PART + g * COL, COL)
-            made[tick, :, pl.ds(start, COL)] = result[g]
+            results[0, tick, :, pl.ds(start, COL)] = result[g]
 
         @pl.when(tick == 0)
         def _():
@@ -468,7 +467,7 @@
             gain_row = gain[:, b * COL : (b + 1) * COL].astype(F32)
             result = cblk[tick, b].astype(F32) + inverse * (gain_row * dn[b])
             result = (result - sblk[tick, b].astype(F32) * factor).astype(BF)
-            grad[tick, :, b * COL : (b + 1) * COL] = result
+            results[1, tick, :, b * COL : (b + 1) * COL] = result
             perm_out[1, b] = result
 
         @pl.when(tick == 0)
@@ -589,7 +588,7 @@
     vmem = pl.BlockSpec(memory_space=pltpu.VMEM)
     hbm = pl.BlockSpec(memory_space=pltpu.HBM)
     rows = XN * SLOTS
-    out = jax.ShapeDtypeStruct((TICKS, tokens, width), BF)
+    out = jax.ShapeDtypeStruct((2, TICKS, tokens, width), BF)
     token_blocks = (blocks, tokens, COL)
     z_block = (parts, PEERS, SLOTS, COL)
     operands = (
@@ -607,11 +606,11 @@
         w_up[0].reshape(parts, PART, hidden_units),
         w_down[0],
     )
-    made, grad = pl.pallas_call(
+    results = pl.pallas_call(
         functools.partial(kernel, parts),
-        out_shape=(out, out),
+        out_shape=out,
         in_specs=[hbm] * 13,
-        out_specs=(vmem, vmem),
+        out_specs=vmem,
         scratch_shapes=[
             pltpu.VMEM((tokens, width), BF),
             pltpu.VMEM((tokens, width), BF),
@@ -663,7 +662,7 @@
         ),
         name="relay",
     )(*[pltpu.with_memory_space_constraint(v, pltpu.HBM) for v in operands])
-    return (made[:, None], grad[:, None])
+    return (results[0][:, None], results[1][:, None])
 
 
 def solution(mesh):

time: 187 us -> 187 us (level)
  no operation moved by 1% of the time
where the time goes in v3:
time: 187 us; the launch traced here: 186 us
  Pallas kernels  185 us (99%)
    pallas_call x1, Pallas kernels, body(): pl.pallas_call(functools.partial(kernel, parts), out_shape=out, in_specs=...  185 us

profile of v3, /device:TPU:1, one launch (start us, length us, event | category | flops | bytes accessed | tf_op | source)
XLA Modules:
  0.0 186.5 jit_solution(1599492552642460625)
XLA Ops:
  0.6 184.8 %relay.1 = bf16[2,2,32,3584]{3,2,1,0:T(8,128)(2,1)S(1)} custom-call(bf16[32,3584]{1,0:T(8,128)(2,1)} %bitcast.30, bf16[32,3584]{1,0:T(8,128)(2,1)} %enter_a_hbm.1, bf16[2,32,3584]{2,1,0:T(8,128)(2,1)} %bitcast.29, bf16[32,3584]{1,0:T(8,128)(2,1)} %bitcast.31, bf16[32,3584]{1,0:T(8,128)(2,1)} %enter_g_hbm.1, bf16[1,3584]{1,0:T(2,128)(2,1)} %gain_hbm.1, ...), custom_call_target="tpu_custom_call" | custom-call | tf_op jit(solution)/shard_map/relay/pallas_call | solution.py:609
  185.5 1.0 slice_bitcast_fusion
